TPU v7x, 32 devices: a whole 2x2x4 slice. The times are simulated.
32 devices in a mesh: groups: 2 (over x), tensor: 16 (over z, y, core).
Axes of the slice: x: 2, y: 2, z: 4, core: 2. Of those that a mesh axis runs over, the one named last changes fastest.
Arguments:
- hidden_in: bfloat16 [4, 32, 12288], P(None, ('groups', 'tensor')), parts along dimension 1, may hold values from -6 to 6
- active: int32 [4, 32, 4], P(None, ('groups', 'tensor')), parts along dimension 1, may hold values from 0 to 31, as said below
- ln_gain: float32 [12288], replicated, may hold values from 0.1 to 1.9
- ln_bias: float32 [12288], replicated, may hold values from -2 to 2
- up_weight: bfloat16 [12288, 4096], P(None, 'tensor'), may hold values from -0.0546875 to 0.0546875
- up_bias: float32 [4096], P('tensor'), may hold values from -3 to 3
- down_weight: bfloat16 [4096, 12288], P('tensor'), may hold values from -0.25 to 0.25
- down_bias: float32 [12288], replicated, may hold values from -3 to 3
Outputs:
- mixed: bfloat16 [4, 32, 12288], P(None, ('groups', 'tensor')), parts along dimension 1
There are 2 independent parts, one for each index of `groups`. A program takes and returns all parts, laid end to end along the dimension named above; an argument that names none is the same for every part. Nothing has to cross between parts.
Inputs may be any that keep to these rules, and one draw needn't show every extreme that they name: `active`: the 4 block ids of a row are distinct. Among the 4 rows that one index of tensor holds, at most 2 name blocks of any one index of tensor (block id // 2), and some index of tensor is named by exactly 2 of them in every draw.
All inputs are finite; a program needn't handle non-finite values.
Results may differ from a plain program's by a relative error of at most 0.0045.
Values may be sent and summed in bfloat16 or wider, within the bound.
A program may use at most 128 MiB of HBM per device.

v0:
```python
import jax
import jax.numpy as jnp
from jax import lax
from jax.sharding import PartitionSpec as P

BLOCK = 128


def layer_norm(inputs, gain, shift):
    center = inputs - jnp.mean(inputs, axis=-1, keepdims=True)
    spread = jnp.mean(center * center, axis=-1, keepdims=True)
    return (center * lax.rsqrt(spread + 1e-05) * gain + shift).astype(jnp.bfloat16)


def block_hits(lists, count):
    wanted = jnp.arange(count, dtype=jnp.int32)
    return jnp.any(lists[..., :, None] == wanted, axis=-2)


def slot_table(hits, capacity):
    device_hit = jnp.any(hits, axis=-1)
    slot_of = jnp.cumsum(device_hit.astype(jnp.int32), axis=0) - 1
    slot_ids = jnp.arange(capacity, dtype=jnp.int32)
    chosen = (slot_of.T[:, None, :] == slot_ids[None, :, None]) & device_hit.T[:, None, :]
    flags = jnp.any(chosen[:, :, :, None] & jnp.transpose(hits, (1, 0, 2))[:, None, :, :], axis=2)
    return (chosen, flags)


def local(hidden_in, active, ln_gain, ln_bias, up_weight, up_bias, down_weight, down_bias):
    n_dev = lax.axis_size("tensor")
    width = hidden_in.shape[2]
    per_dev = up_weight.shape[1] // BLOCK
    row_count = hidden_in.shape[0] * hidden_in.shape[1]
    capacity = row_count // 2
    inputs = hidden_in.reshape(row_count, width).astype(jnp.float32)
    normed = layer_norm(inputs, ln_gain, ln_bias)
    lists = active.reshape(row_count, -1)
    own_hits = block_hits(lists, n_dev * per_dev).reshape(row_count, n_dev, per_dev)
    own_chosen, own_flags = slot_table(own_hits, capacity)
    send_rows = jnp.einsum(
        "dcr,rf->dcf", own_chosen.astype(jnp.bfloat16), normed, preferred_element_type=jnp.float32
    ).astype(jnp.bfloat16)
    send_flags = own_flags.astype(jnp.int32)
    rows = lax.all_to_all(send_rows, "tensor", split_axis=0, concat_axis=0, tiled=True)
    flat = rows.reshape(-1, width)
    pre = jnp.dot(flat, up_weight, preferred_element_type=jnp.float32) + up_bias
    pre = pre.reshape(flat.shape[0], per_dev, BLOCK)
    keep = (
        lax.all_to_all(send_flags, "tensor", split_axis=0, concat_axis=0, tiled=True) > 0
    ).reshape(flat.shape[0], per_dev)[:, :, None]
    hidden = jnp.where(keep, jax.nn.relu(pre), 0.0).reshape(flat.shape[0], -1).astype(jnp.bfloat16)
    partial_rows = jnp.dot(hidden, down_weight, preferred_element_type=jnp.float32).reshape(
        rows.shape
    )
    returned = lax.all_to_all(partial_rows, "tensor", split_axis=0, concat_axis=0, tiled=True)
    total = jnp.einsum(
        "dcr,dcf->rf", own_chosen.astype(jnp.float32), returned, precision=lax.Precision.HIGHEST
    )
    return (inputs + down_bias + total).astype(jnp.bfloat16).reshape(hidden_in.shape)


def solution(mesh):
    in_specs = (
        P(None, ("groups", "tensor"), None),
        P(None, ("groups", "tensor"), None),
        P(),
        P(),
        P(None, "tensor"),
        P("tensor"),
        P("tensor", None),
        P(),
    )
    out_specs = P(None, ("groups", "tensor"), None)
    return jax.shard_map(local, mesh=mesh, in_specs=in_specs, out_specs=out_specs, check_vma=False)
```

profile of v0, /device:TPU:0, one launch (start us, length us, event | category | flops | bytes accessed | tf_op | source)
XLA Modules:
  0.0 92.9 jit_solution(8281419137165108199)
XLA Ops:
  0.0 0.8 fusion.24
  0.8 0.1 reshape.43
  0.9 0.1 reduce_or.28
  1.0 0.1 copy.32
  1.2 0.7 copy.33
  1.9 7.4 %all-to-all-start = ((s32[16,2,2]{1,2,0:T(2,128)}), s32[16,2,2]{1,2,0:T(2,128)S(1)}, u32[]{:S(2)}, u32[]{:S(2)}) async-start(s32[16,2,2]{1,2,0:T(2,128)} %copy.33), calls=%async_computation | async-start | bytes 32768 | tf_op jit(solution)/shard_map/all_to_all | solution.py:49
  9.3 1.1 %convert_reduce_fusion = f32[4]{0:T(128)S(1)} fusion(bf16[4,1,12288]{2,0,1:T(4,128)(2,1)} %param.8), kind=kLoop, calls=%fused_computation.12 | loop fusion | flops 98300 | bytes 98320 | tf_op jit(solution)/shard_map/reduce_sum | solution.py:10
  10.4 1.2 %fusion.13 = f32[4]{0:T(128)S(1)} fusion(bf16[4,1,12288]{2,0,1:T(4,128)(2,1)} %param.8, f32[4]{0:T(128)S(1)} %broadcast_multiply_fusion), kind=kLoop, calls=%fused_computation.18 | loop fusion | flops 196604 | bytes 98336 | tf_op jit(solution)/shard_map/reduce_sum | solution.py:11
  11.6 1.4 %convolution_convert_fusion = bf16[16,2,12288]{2,0,1:T(8,128)(2,1)S(1)} fusion(pred[16,2,4]{0,2,1:T(4,128)(4,1)S(1)} %fusion.25, bf16[4,1,12288]{2,0,1:T(4,128)(2,1)} %param.8, f32[12288]{0:T(1024)} %param.11, f32[12288]{0:T(1024)} %param.10, f32[4]{0:T(128)S(1)} %add_rsqrt_fusion, f32[4]{0:T(128)S(1)} %broadcast_multiply_fusion), kind=kOutput, calls=%fused_computation | convolution fusion | flops 3833856 | bytes 983200 | tf_op jit(solution)/shard_map/dcr,rf->dcf/dot_general | solution.py:40
  13.0 1.7 %copy.37 = bf16[16,2,12288]{2,1,0:T(2,128)(2,1)} copy(bf16[16,2,12288]{2,0,1:T(8,128)(2,1)S(1)} %convolution_convert_fusion) | data formatting | bytes 1572864 | tf_op jit(solution)/shard_map/convert_element_type | solution.py:42
  14.7 0.0 copy-start.2
  14.7 1.1 %all-to-all-done = s32[16,2,2]{1,2,0:T(2,128)S(1)} async-done(((s32[16,2,2]{1,2,0:T(2,128)}), s32[16,2,2]{1,2,0:T(2,128)S(1)}, u32[]{:S(2)}, u32[]{:S(2)}) %all-to-all-start) | async-done | bytes 288 | tf_op jit(solution)/shard_map/all_to_all | solution.py:49
  15.8 5.0 %all-to-all-start.1 = ((bf16[16,2,12288]{2,1,0:T(2,128)(2,1)}), bf16[16,2,12288]{2,1,0:T(2,128)(2,1)S(1)}, u32[]{:S(2)}, u32[]{:S(2)}) async-start(bf16[16,2,12288]{2,1,0:T(2,128)(2,1)} %copy.37), calls=%async_computation.1 | async-start | bytes 1572864 | tf_op jit(solution)/shard_map/all_to_all | solution.py:44
  20.9 0.1 copy.34
  21.0 0.1 copy.35
  21.1 0.1 broadcast_in_dim.10
  21.2 0.1 copy.36
  21.3 18.3 %all-to-all-done.1 = bf16[16,2,12288]{2,1,0:T(2,128)(2,1)S(1)} async-done(((bf16[16,2,12288]{2,1,0:T(2,128)(2,1)}), bf16[16,2,12288]{2,1,0:T(2,128)(2,1)S(1)}, u32[]{:S(2)}, u32[]{:S(2)}) %all-to-all-start.1) | async-done | bytes 786464 | tf_op jit(solution)/shard_map/all_to_all | solution.py:44
  39.6 0.3 reshape.44
  39.9 0.1 broadcast_in_dim.11
  40.0 0.0 copy-done.2
  40.0 4.0 %fusion.8 = bf16[32,256]{1,0:T(8,128)(2,1)S(1)} fusion(bf16[32,12288]{1,0:T(8,128)(2,1)S(1)} %reshape.44, bf16[12288,256]{1,0:T(8,128)(2,1)} %param.12, pred[4,8,2,128]{3,2,1,0:T(4,128)(4,1)S(1)} %bitcast.54, f32[256]{0:T(256)S(1)} %copy-done.2), kind=kOutput, calls=%fused_computation.11 | convolution fusion | flops 201359360 | bytes 7103488 | tf_op jit(solution)/shard_map/dot_general | solution.py:46
  44.0 4.0 %fusion.3 = f32[16,2,12288]{2,0,1:T(8,128)S(1)} fusion(bf16[256,12288]{1,0:T(8,128)(2,1)} %param.14, bf16[16,2,256]{2,1,0:T(2,128)(2,1)S(1)} %dot_general.16), kind=kOutput, calls=%fused_computation.5 | convolution fusion | flops 201326592 | bytes 7880704 | tf_op jit(solution)/shard_map/dot_general | solution.py:52
  47.9 1.2 %copy.39 = f32[16,2,12288]{2,1,0:T(2,128)S(1)} copy(f32[16,2,12288]{2,0,1:T(8,128)S(1)} %fusion.3) | data formatting | bytes 3145728 | tf_op jit(solution)/shard_map/dot_general | solution.py:52
  49.2 0.0 copy-start
  49.2 0.0 copy-start.1
  49.2 41.5 %all_to_all.15 = f32[16,2,12288]{2,1,0:T(2,128)S(1)} all-to-all(f32[16,2,12288]{2,1,0:T(2,128)S(1)} %copy.39), channel_id=1, replica_groups=mesh['groups'=2,'tensor'=16] {'tensor'}, dimensions={0} | all-to-all | bytes 3145728 | tf_op jit(solution)/shard_map/all_to_all | solution.py:55
  90.7 0.0 copy-done
  90.7 0.0 copy-done.1
  90.7 2.2 %fusion.2 = bf16[4,1,12288]{2,0,1:T(4,128)(2,1)} fusion(pred[16,2,4]{0,2,1:T(4,128)(4,1)S(1)} %fusion.25, f32[16,2,12288]{2,1,0:T(2,128)S(1)} %all_to_all.15, bf16[4,1,12288]{2,0,1:T(4,128)(2,1)S(1)} %copy-done, f32[12288]{0:T(1024)S(1)} %copy-done.1), kind=kOutput, calls=%fused_computation.4 | convolution fusion | flops 19070976 | bytes 1818752 | tf_op jit(solution)/shard_map/dcr,dcf->rf/dot_general | solution.py:56
  (10 shorter events, 0.1 us)
Async XLA Ops:
  1.9 13.9 %all-to-all-start = ((s32[16,2,2]{1,2,0:T(2,128)}), s32[16,2,2]{1,2,0:T(2,128)S(1)}, u32[]{:S(2)}, u32[]{:S(2)}) async-start(s32[16,2,2]{1,2,0:T(2,128)} %copy.33), calls=%async_computation | async-start | bytes 32768 | tf_op jit(solution)/shard_map/all_to_all | solution.py:49
  14.7 25.3 %copy-start.2 = (f32[256]{0:T(256)S(1)}, f32[256]{0:T(256)}, u32[]{:S(2)}) copy-start(f32[256]{0:T(256)} %param.13) | copy-start | bytes 3076
  15.8 23.7 %all-to-all-start.1 = ((bf16[16,2,12288]{2,1,0:T(2,128)(2,1)}), bf16[16,2,12288]{2,1,0:T(2,128)(2,1)S(1)}, u32[]{:S(2)}, u32[]{:S(2)}) async-start(bf16[16,2,12288]{2,1,0:T(2,128)(2,1)} %copy.37), calls=%async_computation.1 | async-start | bytes 1572864 | tf_op jit(solution)/shard_map/all_to_all | solution.py:44
  49.2 41.5 %copy-start = (bf16[4,1,12288]{2,0,1:T(4,128)(2,1)S(1)}, bf16[4,1,12288]{2,0,1:T(4,128)(2,1)}, u32[]{:S(2)}) copy-start(bf16[4,1,12288]{2,0,1:T(4,128)(2,1)} %param.8) | copy-start | bytes 294916
  49.2 41.5 %copy-start.1 = (f32[12288]{0:T(1024)S(1)}, f32[12288]{0:T(1024)}, u32[]{:S(2)}) copy-start(f32[12288]{0:T(1024)} %param.15) | copy-start | bytes 147460
where the time goes:
time: 93.7 us; the launch traced here: 92.9 us
  blocking collectives  41.5 us (44%)
  waiting for transfers between devices  19.4 us (21%)
  starting transfers between devices  12.4 us (13%)
  matrix products  11.5 us (12%)
  local copies, waits for them, and re-layouts  4.64 us (5%)
  other arithmetic  3.32 us (4%)
    all_to_all x1, blocking collectives, local(): lax.all_to_all(partial_rows, 'tensor', split_axis=0, concat_axis=0, tiled...  41.5 us
    all_to_all x1, waiting for transfers between devices, local(): lax.all_to_all(send_rows, 'tensor', split_axis=0, concat_axis=0, tiled=True)  18.3 us
    all_to_all x1, starting transfers between devices, local(): lax.all_to_all(send_flags, 'tensor', split_axis=0, concat_axis=0, tiled=T...  7.39 us
    all_to_all x1, starting transfers between devices, local(): lax.all_to_all(send_rows, 'tensor', split_axis=0, concat_axis=0, tiled=True)  5.03 us
    dot_general x1, matrix products, local(): pre = jnp.dot(flat, up_weight, preferred_element_type=jnp.float32) + up_bias  3.97 us
    dot_general x1, matrix products, local(): jnp.dot(hidden, down_weight, preferred_element_type=jnp.float32)  3.96 us
    dot_general x1, matrix products, local(): jnp.einsum('dcr,dcf->rf', own_chosen.astype(jnp.float32), returned, preci...  2.16 us
  transfers between devices with their start and end apart: 2, of which 2 were waited for; matrix products, arithmetic and copies ran while one was open for 6% of the time, Pallas kernels for 0%

commit v1 on v0

v1 whole, which is shorter than its diff:
```python
import functools
import math

import jax
import jax.numpy as jnp
from jax import lax
from jax.experimental import pallas as pl
from jax.experimental.pallas import tpu as pltpu
from jax.sharding import PartitionSpec as P

BLOCK = 128
LANES = 128
PACK = 16
PARTS = 4


def sizes(n_dev):
    cores = 2 if n_dev % 2 == 0 else 1
    rest = n_dev // cores
    mids = math.isqrt(rest)
    while rest % mids:
        mids -= 1
    return rest // mids, mids, cores


def kernel(n_dev, hid, act, gain, shift, up_bias, down_bias, up_hbm, down_hbm, out,
           rows, w_up, w_down, acc, hid_cat, core_in, mid_out, mid_own, mid_in, far_out, far_own, far_in,
           up_sem, down_sem, far_s, far_r, mid_s, mid_r, core_s, core_r,
           rcore_s, rcore_r, rmid_s, rmid_r, rfar_s, rfar_r):
    fars, mids, cores = sizes(n_dev)
    row_count, width = hid.shape
    split = PACK // row_count
    part = width // split
    step = part // PARTS
    units = w_up.shape[2]
    per_dev = units // BLOCK

    me = lax.axis_index("tensor")
    core = lax.rem(me, cores)
    mid = lax.rem(me // cores, mids)
    far = me // (cores * mids)

    def device(c, m, f):
        return {"tensor": (f * mids + m) * cores + c}

    def place(c, m, f):
        return (c * mids + m) * fars + f

    far_peers = [(d, device(core, mid, lax.rem(far + d, fars))) for d in range(1, fars)]
    mid_peers = [(d, device(core, lax.rem(mid + d, mids), far)) for d in range(1, mids)]
    core_peers = [(d, device(lax.rem(core + d, cores), mid, far)) for d in range(1, cores)]
    barrier = pltpu.get_barrier_semaphore()
    for _, peer in far_peers + mid_peers + core_peers:
        pl.semaphore_signal(barrier, inc=1, device_id=peer, device_id_type=pl.DeviceIdType.MESH)

    up_copies, down_copies = [], []
    for c in range(PARTS):
        copy = pltpu.make_async_copy(
            up_hbm.at[:, pl.ds(c * step, step), :], w_up.at[:, pl.ds(c * step, step), :], up_sem.at[c])
        copy.start()
        up_copies.append(copy)

    def remote(src, dst, send, recv, peer):
        copy = pltpu.make_async_remote_copy(
            src_ref=src, dst_ref=dst, send_sem=send, recv_sem=recv,
            device_id=peer, device_id_type=pl.DeviceIdType.MESH)
        copy.start()
        return copy

    x = hid[...].astype(jnp.float32)
    mean = jnp.mean(x, axis=-1, keepdims=True)
    center = x - mean
    scale = lax.rsqrt(jnp.mean(center * center, axis=-1, keepdims=True) + 1e-05)

    mine = place(core, mid, far)
    lane = lax.broadcasted_iota(jnp.int32, (row_count, LANES), 1)
    ids = jnp.full((row_count, LANES), -1, jnp.int32)
    for a in range(act.shape[1]):
        ids = jnp.where(lane == a, act[:, a:a + 1], ids)
    ids = ids.astype(jnp.float32)
    rows[mine, :, 0:LANES] = jnp.concatenate([ids] * split, axis=0).astype(jnp.bfloat16)

    def spans(c):
        start = 0 if c == 0 else LANES + c * step
        return pl.ds(start, step + (LANES if c == 0 else 0))

    def norm_part(c):
        pieces = []
        for q in range(split):
            at = q * part + c * step
            piece = (hid[:, at:at + step].astype(jnp.float32) - mean) * scale
            pieces.append(piece * gain[:, at:at + step] + shift[:, at:at + step])
        rows[mine, :, LANES + c * step:LANES + (c + 1) * step] = jnp.concatenate(pieces, axis=0).astype(jnp.bfloat16)

    far_copies, mid_copies, core_copies = [], [], []
    for c in range(PARTS):
        norm_part(c)
        if c == 0:
            pl.semaphore_wait(barrier, fars + mids + cores - 3)
        here = rows.at[mine, :, spans(c)]
        far_copies.append([remote(here, here, far_s.at[c, d], far_r.at[c, d], peer) for d, peer in far_peers])

    for c in range(PARTS):
        for q in range(split):
            at = pl.ds(q * part + c * step, step)
            copy = pltpu.make_async_copy(down_hbm.at[:, at], w_down.at[:, at], down_sem.at[c, q])
            copy.start()
            down_copies.append(copy)

    tile = min(n_dev, 16)
    tiles = n_dev // tile
    tall = tile * PACK

    def over_tiles(body):
        if tiles == 1:
            body(0)
        else:
            pl.loop(0, tiles)(body)

    def row_part(shape):
        return (lax.broadcasted_iota(jnp.int32, shape, 0) // row_count) % split

    def up_part(c):
        up_copies[c].wait()

        def body(t):
            got = rows[pl.ds(t * tile, tile), :, LANES + c * step:LANES + (c + 1) * step].reshape(tall, step)
            which = row_part((tall, units))
            total = jnp.zeros((tall, units), jnp.float32)
            for q in range(split):
                piece = jnp.dot(got, w_up[q, c * step:(c + 1) * step, :], preferred_element_type=jnp.float32)
                total = total + jnp.where(which == q, piece, 0.0)
            at = pl.ds(pl.multiple_of(t * tall, tall), tall)
            if c == 0:
                acc[at, :] = total
            else:
                acc[at, :] += total

        over_tiles(body)

    for s in range(PARTS + 2):
        if s < PARTS:
            for copy in far_copies[s]:
                copy.wait_recv()
            here = rows.at[pl.ds(place(core, mid, 0), fars), :, spans(s)]
            mid_copies.append([remote(here, here, mid_s.at[s, d], mid_r.at[s, d], peer) for d, peer in mid_peers])
        if 0 <= s - 1 < PARTS:
            c = s - 1
            for copy in mid_copies[c]:
                copy.wait_recv()
            here = rows.at[pl.ds(place(core, 0, 0), fars * mids), :, spans(c)]
            core_copies.append([remote(here, here, core_s.at[c, d], core_r.at[c, d], peer) for d, peer in core_peers])
        if 0 <= s - 2:
            c = s - 2
            for copy in core_copies[c]:
                copy.wait_recv()
            up_part(c)

    def hidden_part(t):
        at = pl.ds(pl.multiple_of(t * tall, tall), tall)
        total = acc[at, :].reshape(tile, 2, 8, units)
        total = total[:, 0] + total[:, 1]
        if split == 4:
            total = total + pltpu.roll(total, row_count, 1)
        total = jnp.concatenate([total[:, None], total[:, None]], axis=1).reshape(tall, units)
        value = jnp.maximum(total + up_bias[...], 0.0)
        named = rows[pl.ds(t * tile, tile), :, 0:LANES].reshape(tall, LANES).astype(jnp.float32)
        kept = []
        for b in range(per_dev):
            wanted = (me * per_dev + b).astype(jnp.float32)
            hit = jnp.max(jnp.where(named == wanted, 1.0, 0.0), axis=1, keepdims=True)
            kept.append(jnp.where(hit > 0.0, value[:, b * BLOCK:(b + 1) * BLOCK], 0.0))
        value = jnp.concatenate(kept, axis=1)
        which = row_part((tall, units))
        for q in range(split):
            hid_cat[at, q * units:(q + 1) * units] = jnp.where(which == q, value, 0.0).astype(jnp.bfloat16)

    over_tiles(hidden_part)
    for copies in far_copies + mid_copies + core_copies:
        for copy in copies:
            copy.wait_send()

    def down_part(c):
        for q in range(split):
            down_copies[c * split + q].wait()

        def body(t):
            at = pl.ds(pl.multiple_of(t * tall, tall), tall)
            total = jnp.zeros((tall, step), jnp.float32)
            for q in range(split):
                start = q * part + c * step
                total = total + jnp.dot(hid_cat[at, q * units:(q + 1) * units], w_down[:, start:start + step],
                                        preferred_element_type=jnp.float32)
            rows[pl.ds(t * tile, tile), :, LANES + c * step:LANES + (c + 1) * step] = (
                total.astype(jnp.bfloat16).reshape(tile, PACK, step))

        over_tiles(body)

    back_core, back_mid, back_far = [], [], []
    plane = fars * mids
    for s in range(PARTS + 3):
        if s < PARTS:
            c = s
            down_part(c)
            cols = pl.ds(LANES + c * step, step)
            back_core.append([
                remote(rows.at[pl.ds(place(lax.rem(core + d, cores), 0, 0), plane), :, cols],
                       core_in.at[d - 1, :, :, pl.ds(c * step, step)], rcore_s.at[c, d], rcore_r.at[c, d], peer)
                for d, peer in core_peers])
        if 0 <= s - 1 < PARTS:
            c = s - 1
            for copy in back_core[c]:
                copy.wait_recv()
            cs = slice(c * step, (c + 1) * step)

            def chip_sum(m):
                total = rows[pl.ds(place(core, m, 0), fars), :, LANES + c * step:LANES + (c + 1) * step]
                total = total.astype(jnp.float32)
                for d in range(1, cores):
                    total = total + core_in[d - 1, pl.ds(m * fars, fars), :, cs].astype(jnp.float32)
                return total

            for d in range(1, mids):
                mid_out[d - 1, :, :, cs] = chip_sum(lax.rem(mid + d, mids)).astype(jnp.bfloat16)
            back_mid.append([
                remote(mid_out.at[d - 1, :, :, pl.ds(c * step, step)], mid_in.at[d - 1, :, :, pl.ds(c * step, step)],
                       rmid_s.at[c, d], rmid_r.at[c, d], peer)
                for d, peer in mid_peers])
            mid_own[:, :, cs] = chip_sum(mid)
        if 0 <= s - 2 < PARTS:
            c = s - 2
            for copy in back_mid[c]:
                copy.wait_recv()
            cs = slice(c * step, (c + 1) * step)

            def line_sum(f):
                total = mid_own[f, :, cs]
                for d in range(1, mids):
                    total = total + mid_in[d - 1, f, :, cs].astype(jnp.float32)
                return total

            for d in range(1, fars):
                far_out[d - 1, :, cs] = line_sum(lax.rem(far + d, fars)).astype(jnp.bfloat16)
            back_far.append([
                remote(far_out.at[d - 1, :, pl.ds(c * step, step)], far_in.at[d - 1, :, pl.ds(c * step, step)],
                       rfar_s.at[c, d], rfar_r.at[c, d], peer)
                for d, peer in far_peers])
            far_own[:, cs] = line_sum(far)
        if 0 <= s - 3:
            c = s - 3
            for copy in back_far[c]:
                copy.wait_recv()
            cs = slice(c * step, (c + 1) * step)
            total = far_own[:, cs]
            for d in range(1, fars):
                total = total + far_in[d - 1, :, cs].astype(jnp.float32)
            for q in range(split):
                at = slice(q * part + c * step, q * part + (c + 1) * step)
                mixed = hid[:, at].astype(jnp.float32) + down_bias[:, at] + total[q * row_count:(q + 1) * row_count]
                out[:, at] = mixed.astype(out.dtype)
    for copies in back_core + back_mid + back_far:
        for copy in copies:
            copy.wait_send()


def local(n_dev, hidden_in, active, ln_gain, ln_bias, up_weight, up_bias, down_weight, down_bias):
    fars, mids, cores = sizes(n_dev)
    width = hidden_in.shape[2]
    row_count = hidden_in.shape[0] * hidden_in.shape[1]
    split = PACK // row_count
    part = width // split
    units = up_weight.shape[1]
    plane = fars * mids
    vmem = pl.BlockSpec(memory_space=pltpu.VMEM)
    hbm = pl.BlockSpec(memory_space=pl.ANY)
    dma = pltpu.SemaphoreType.DMA
    bf16, f32 = jnp.bfloat16, jnp.float32
    out = pl.pallas_call(
        functools.partial(kernel, n_dev),
        out_shape=jax.ShapeDtypeStruct((row_count, width), bf16),
        in_specs=[vmem] * 6 + [hbm] * 2,
        out_specs=vmem,
        scratch_shapes=[
            pltpu.VMEM((n_dev, PACK, LANES + part), bf16),
            pltpu.VMEM((split, part, units), bf16),
            pltpu.VMEM((units, width), bf16),
            pltpu.VMEM((n_dev * PACK, units), f32),
            pltpu.VMEM((n_dev * PACK, split * units), bf16),
            pltpu.VMEM((max(cores - 1, 1), plane, PACK, part), bf16),
            pltpu.VMEM((max(mids - 1, 1), fars, PACK, part), bf16),
            pltpu.VMEM((fars, PACK, part), f32),
            pltpu.VMEM((max(mids - 1, 1), fars, PACK, part), bf16),
            pltpu.VMEM((max(fars - 1, 1), PACK, part), bf16),
            pltpu.VMEM((PACK, part), f32),
            pltpu.VMEM((max(fars - 1, 1), PACK, part), bf16),
            dma((PARTS,)), dma((PARTS, split)),
            dma((PARTS, fars)), dma((PARTS, fars)),
            dma((PARTS, mids)), dma((PARTS, mids)),
            dma((PARTS, cores)), dma((PARTS, cores)),
            dma((PARTS, cores)), dma((PARTS, cores)),
            dma((PARTS, mids)), dma((PARTS, mids)),
            dma((PARTS, fars)), dma((PARTS, fars)),
        ],
        compiler_params=pltpu.CompilerParams(
            collective_id=0, has_side_effects=True, vmem_limit_bytes=60 * 1024 * 1024),
    )(
        hidden_in.reshape(row_count, width), active.reshape(row_count, -1),
        ln_gain.reshape(1, -1), ln_bias.reshape(1, -1), up_bias.reshape(1, -1), down_bias.reshape(1, -1),
        up_weight.reshape(split, part, units), down_weight,
    )
    return out.reshape(hidden_in.shape)


def solution(mesh):
    in_specs = (
        P(None, ("groups", "tensor"), None),
        P(None, ("groups", "tensor"), None),
        P(),
        P(),
        P(None, "tensor"),
        P("tensor"),
        P("tensor", None),
        P(),
    )
    out_specs = P(None, ("groups", "tensor"), None)
    return jax.shard_map(
        functools.partial(local, mesh.shape["tensor"]), mesh=mesh, in_specs=in_specs, out_specs=out_specs,
        check_vma=False)
```

time: 93.7 us -> 47.8 us (0.51)
  Pallas kernels: 0 us -> 46 us
  blocking collectives: 41.5 us -> 0 us
  waiting for transfers between devices: 19.4 us -> 0 us
  starting transfers between devices: 12.4 us -> 0 us
  matrix products: 11.5 us -> 0 us
  other arithmetic: 3.32 us -> 0 us
  local copies, waits for them, and re-layouts: 4.64 us -> 1.57 us
    pallas_call x0 -> x1, Pallas kernels: none -> 46 us  [local(): pl.pallas_call(functools.partial(kernel, n_dev), out_shape=jax.ShapeDtype...]
    all_to_all x1 -> x0, blocking collectives: 41.5 us -> none  [local(): lax.all_to_all(partial_rows, 'tensor', split_axis=0, concat_axis=0, tiled...]
    all_to_all x2 -> x0, waiting for transfers between devices: 19.4 us -> none  [the longest x1 18.3 us: local(): lax.all_to_all(send_rows, 'tensor', split_axis=0, concat_axis=0, tiled=True)]
    all_to_all x2 -> x0, starting transfers between devices: 12.4 us -> none  [the longest x1 7.39 us: local(): lax.all_to_all(send_flags, 'tensor', split_axis=0, concat_axis=0, tiled=T...]
    dot_general x4 -> x0, matrix products: 11.5 us -> none  [the longest x1 3.97 us: local(): pre = jnp.dot(flat, up_weight, preferred_element_type=jnp.float32) + up_bias]
    convert_element_type x2 -> x0, local copies, waits for them, and re-layouts: 2.38 us -> none  [the longest x1 1.69 us: local(): send_rows = jnp.einsum('dcr,rf->dcf', own_chosen.astype(jnp.bfloat16), no...]
    reduce_sum x2 -> x0, other arithmetic: 2.28 us -> none  [the longest x1 1.18 us: layer_norm(): spread = jnp.mean(center * center, axis=-1, keepdims=True)]
    unnamed x6 -> x1, local copies, waits for them, and re-layouts: 0.02 us -> 1.57 us
  transfers between devices with their start and end apart: 2 -> 0, of which waited for: 2 -> 0; matrix products, arithmetic and copies ran while one was open for 6% -> 0% of each run, Pallas kernels for 0% -> 0%
where the time goes in v1:
time: 47.8 us; the launch traced here: 47.6 us
  Pallas kernels  46 us (96%)
  local copies, waits for them, and re-layouts  1.57 us (3%)
    pallas_call x1, Pallas kernels, local(): pl.pallas_call(functools.partial(kernel, n_dev), out_shape=jax.ShapeDtype...  46 us
    unnamed x1, local copies, waits for them, and re-layouts  1.57 us

profile of v1, /device:TPU:0, one launch (start us, length us, event | category | flops | bytes accessed | tf_op | source)
XLA Modules:
  0.0 47.6 jit_solution(3803934684479731394)
XLA Ops:
  0.0 46.0 %shard_map.82 = bf16[4,12288]{1,0:T(4,128)(2,1)} custom-call(bf16[4,12288]{1,0:T(4,128)(2,1)} %bitcast.10, s32[4,4]{1,0:T(4,128)} %bitcast.14, f32[1,12288]{1,0:T(1,128)} %bitcast.11, f32[1,12288]{1,0:T(1,128)} %bitcast.12, f32[1,256]{1,0:T(1,128)} %bitcast.15, f32[1,12288]{1,0:T(1,128)} %bitcast.13, bf16[4,3072,256]{2,1,0:T(8,128)(2,1)} %bitcast.8, ...), custom_call_target="tpu_custom_call" | custom-call | tf_op jit(solution)/shard_map/pallas_call | solution.py:278
  46.0 1.6 %copy.10 = bf16[4,1,12288]{2,0,1:T(4,128)(2,1)} copy(bf16[4,1,12288]{2,0,1:T(4,128)(2,1)} %bitcast.9) | data formatting | bytes 196608

commit v2 on v1

--- a/solution.py
+++ b/solution.py
@@ -11,7 +11,7 @@
 BLOCK = 128
 LANES = 128
 PACK = 16
-PARTS = 4
+PARTS = 2
 
 
 def sizes(n_dev):
@@ -24,7 +24,7 @@
 
 
 def kernel(n_dev, hid, act, gain, shift, up_bias, down_bias, up_hbm, down_hbm, out,
-           rows, w_up, w_down, acc, hid_cat, core_in, mid_out, mid_own, mid_in, far_out, far_own, far_in,
+           rows, w_up, w_down, acc, hid_cat, core_in, mid_out, mid_in, far_out, far_own, far_in,
            up_sem, down_sem, far_s, far_r, mid_s, mid_r, core_s, core_r,
            rcore_s, rcore_r, rmid_s, rmid_r, rfar_s, rfar_r):
     fars, mids, cores = sizes(n_dev)
@@ -46,7 +46,13 @@
     def place(c, m, f):
         return (c * mids + m) * fars + f
 
-    far_peers = [(d, device(core, mid, lax.rem(far + d, fars))) for d in range(1, fars)]
+    def other(d):
+        return jnp.bitwise_xor(far, d) if fars & (fars - 1) == 0 else lax.rem(far + d, fars)
+
+    def source(d):
+        return jnp.bitwise_xor(far, d) if fars & (fars - 1) == 0 else lax.rem(far + fars - d, fars)
+
+    far_peers = [(d, device(core, mid, other(d))) for d in range(1, fars)]
     mid_peers = [(d, device(core, lax.rem(mid + d, mids), far)) for d in range(1, mids)]
     core_peers = [(d, device(lax.rem(core + d, cores), mid, far)) for d in range(1, cores)]
     barrier = pltpu.get_barrier_semaphore()
@@ -92,11 +98,16 @@
             pieces.append(piece * gain[:, at:at + step] + shift[:, at:at + step])
         rows[mine, :, LANES + c * step:LANES + (c + 1) * step] = jnp.concatenate(pieces, axis=0).astype(jnp.bfloat16)
 
-    far_copies, mid_copies, core_copies = [], [], []
+    def spread(c, d):
+        here = rows.at[place(core, mid, source(d) if d else far), :, spans(c)]
+        return [remote(here, here, mid_s.at[c, d, e], mid_r.at[c, d, e], peer) for e, peer in mid_peers]
+
+    far_copies, mid_copies, core_copies = [], [[] for _ in range(PARTS)], []
     for c in range(PARTS):
         norm_part(c)
         if c == 0:
             pl.semaphore_wait(barrier, fars + mids + cores - 3)
+        mid_copies[c] += spread(c, 0)
         here = rows.at[mine, :, spans(c)]
         far_copies.append([remote(here, here, far_s.at[c, d], far_r.at[c, d], peer) for d, peer in far_peers])
 
@@ -138,23 +149,18 @@
 
         over_tiles(body)
 
-    for s in range(PARTS + 2):
-        if s < PARTS:
-            for copy in far_copies[s]:
-                copy.wait_recv()
-            here = rows.at[pl.ds(place(core, mid, 0), fars), :, spans(s)]
-            mid_copies.append([remote(here, here, mid_s.at[s, d], mid_r.at[s, d], peer) for d, peer in mid_peers])
-        if 0 <= s - 1 < PARTS:
-            c = s - 1
-            for copy in mid_copies[c]:
-                copy.wait_recv()
-            here = rows.at[pl.ds(place(core, 0, 0), fars * mids), :, spans(c)]
-            core_copies.append([remote(here, here, core_s.at[c, d], core_r.at[c, d], peer) for d, peer in core_peers])
-        if 0 <= s - 2:
-            c = s - 2
-            for copy in core_copies[c]:
-                copy.wait_recv()
-            up_part(c)
+    for c in range(PARTS):
+        for d in range(1, fars):
+            far_copies[c][d - 1].wait_recv()
+            mid_copies[c] += spread(c, d)
+    for c in range(PARTS):
+        for copy in mid_copies[c]:
+            copy.wait_recv()
+        here = rows.at[pl.ds(place(core, 0, 0), fars * mids), :, spans(c)]
+        core_copies.append([remote(here, here, core_s.at[c, d], core_r.at[c, d], peer) for d, peer in core_peers])
+        for copy in core_copies[c]:
+            copy.wait_recv()
+        up_part(c)
 
     def hidden_part(t):
         at = pl.ds(pl.multiple_of(t * tall, tall), tall)
@@ -196,69 +202,66 @@
 
         over_tiles(body)
 
-    back_core, back_mid, back_far = [], [], []
+    back_core, back_mid, back_far = [], {}, []
     plane = fars * mids
-    for s in range(PARTS + 3):
-        if s < PARTS:
-            c = s
-            down_part(c)
-            cols = pl.ds(LANES + c * step, step)
-            back_core.append([
-                remote(rows.at[pl.ds(place(lax.rem(core + d, cores), 0, 0), plane), :, cols],
-                       core_in.at[d - 1, :, :, pl.ds(c * step, step)], rcore_s.at[c, d], rcore_r.at[c, d], peer)
-                for d, peer in core_peers])
-        if 0 <= s - 1 < PARTS:
-            c = s - 1
-            for copy in back_core[c]:
-                copy.wait_recv()
-            cs = slice(c * step, (c + 1) * step)
-
-            def chip_sum(m):
-                total = rows[pl.ds(place(core, m, 0), fars), :, LANES + c * step:LANES + (c + 1) * step]
-                total = total.astype(jnp.float32)
-                for d in range(1, cores):
-                    total = total + core_in[d - 1, pl.ds(m * fars, fars), :, cs].astype(jnp.float32)
-                return total
-
-            for d in range(1, mids):
-                mid_out[d - 1, :, :, cs] = chip_sum(lax.rem(mid + d, mids)).astype(jnp.bfloat16)
-            back_mid.append([
-                remote(mid_out.at[d - 1, :, :, pl.ds(c * step, step)], mid_in.at[d - 1, :, :, pl.ds(c * step, step)],
-                       rmid_s.at[c, d], rmid_r.at[c, d], peer)
-                for d, peer in mid_peers])
-            mid_own[:, :, cs] = chip_sum(mid)
-        if 0 <= s - 2 < PARTS:
-            c = s - 2
-            for copy in back_mid[c]:
-                copy.wait_recv()
-            cs = slice(c * step, (c + 1) * step)
-
-            def line_sum(f):
-                total = mid_own[f, :, cs]
-                for d in range(1, mids):
-                    total = total + mid_in[d - 1, f, :, cs].astype(jnp.float32)
-                return total
-
-            for d in range(1, fars):
-                far_out[d - 1, :, cs] = line_sum(lax.rem(far + d, fars)).astype(jnp.bfloat16)
-            back_far.append([
-                remote(far_out.at[d - 1, :, pl.ds(c * step, step)], far_in.at[d - 1, :, pl.ds(c * step, step)],
-                       rfar_s.at[c, d], rfar_r.at[c, d], peer)
-                for d, peer in far_peers])
-            far_own[:, cs] = line_sum(far)
-        if 0 <= s - 3:
-            c = s - 3
-            for copy in back_far[c]:
-                copy.wait_recv()
-            cs = slice(c * step, (c + 1) * step)
-            total = far_own[:, cs]
-            for d in range(1, fars):
-                total = total + far_in[d - 1, :, cs].astype(jnp.float32)
-            for q in range(split):
-                at = slice(q * part + c * step, q * part + (c + 1) * step)
-                mixed = hid[:, at].astype(jnp.float32) + down_bias[:, at] + total[q * row_count:(q + 1) * row_count]
-                out[:, at] = mixed.astype(out.dtype)
-    for copies in back_core + back_mid + back_far:
+
+    def chip_sum(c, m, f):
+        at = slice(c * step, (c + 1) * step)
+        total = rows[place(core, m, f), :, LANES + c * step:LANES + (c + 1) * step].astype(jnp.float32)
+        for e in range(1, cores):
+            total = total + core_in[e - 1, m * fars + f, :, at].astype(jnp.float32)
+        return total
+
+    def send_mid(c, d):
+        at = slice(c * step, (c + 1) * step)
+        for e, peer in mid_peers:
+            mid_out[e - 1, d, :, at] = chip_sum(c, lax.rem(mid + e, mids), other(d) if d else far).astype(jnp.bfloat16)
+            cols = pl.ds(c * step, step)
+            back_mid[c, d, e] = remote(mid_out.at[e - 1, d, :, cols], mid_in.at[e - 1, d, :, cols],
+                                       rmid_s.at[c, d, e], rmid_r.at[c, d, e], peer)
+
+    def line_sum(c, d):
+        total = chip_sum(c, mid, other(d) if d else far)
+        for e in range(1, mids):
+            back_mid[c, d, e].wait_recv()
+            total = total + mid_in[e - 1, d, :, c * step:(c + 1) * step].astype(jnp.float32)
+        return total
+
+    for c in range(PARTS):
+        down_part(c)
+        cols = pl.ds(LANES + c * step, step)
+        back_core.append([
+            remote(rows.at[pl.ds(place(lax.rem(core + d, cores), 0, 0), plane), :, cols],
+                   core_in.at[d - 1, :, :, pl.ds(c * step, step)], rcore_s.at[c, d], rcore_r.at[c, d], peer)
+            for d, peer in core_peers])
+    for c in range(PARTS):
+        for copy in back_core[c]:
+            copy.wait_recv()
+        for d in range(1, fars):
+            send_mid(c, d)
+    for c in range(PARTS):
+        send_mid(c, 0)
+    for c in range(PARTS):
+        cs = slice(c * step, (c + 1) * step)
+        for d, peer in far_peers:
+            far_out[d - 1, :, cs] = line_sum(c, d).astype(jnp.bfloat16)
+            cols = pl.ds(c * step, step)
+            back_far.append(remote(far_out.at[d - 1, :, cols], far_in.at[d - 1, :, cols],
+                                   rfar_s.at[c, d], rfar_r.at[c, d], peer))
+    for c in range(PARTS):
+        cs = slice(c * step, (c + 1) * step)
+        far_own[:, cs] = line_sum(c, 0)
+    for c in range(PARTS):
+        cs = slice(c * step, (c + 1) * step)
+        total = far_own[:, cs]
+        for d in range(1, fars):
+            back_far[c * (fars - 1) + d - 1].wait_recv()
+            total = total + far_in[d - 1, :, cs].astype(jnp.float32)
+        for q in range(split):
+            at = slice(q * part + c * step, q * part + (c + 1) * step)
+            mixed = hid[:, at].astype(jnp.float32) + down_bias[:, at] + total[q * row_count:(q + 1) * row_count]
+            out[:, at] = mixed.astype(out.dtype)
+    for copies in back_core + [back_mid.values(), back_far]:
         for copy in copies:
             copy.wait_send()
 
@@ -288,17 +291,16 @@
             pltpu.VMEM((n_dev * PACK, split * units), bf16),
             pltpu.VMEM((max(cores - 1, 1), plane, PACK, part), bf16),
             pltpu.VMEM((max(mids - 1, 1), fars, PACK, part), bf16),
-            pltpu.VMEM((fars, PACK, part), f32),
             pltpu.VMEM((max(mids - 1, 1), fars, PACK, part), bf16),
             pltpu.VMEM((max(fars - 1, 1), PACK, part), bf16),
             pltpu.VMEM((PACK, part), f32),
             pltpu.VMEM((max(fars - 1, 1), PACK, part), bf16),
             dma((PARTS,)), dma((PARTS, split)),
             dma((PARTS, fars)), dma((PARTS, fars)),
-            dma((PARTS, mids)), dma((PARTS, mids)),
+            dma((PARTS, fars, mids)), dma((PARTS, fars, mids)),
             dma((PARTS, cores)), dma((PARTS, cores)),
             dma((PARTS, cores)), dma((PARTS, cores)),
-            dma((PARTS, mids)), dma((PARTS, mids)),
+            dma((PARTS, fars, mids)), dma((PARTS, fars, mids)),
             dma((PARTS, fars)), dma((PARTS, fars)),
         ],
         compiler_params=pltpu.CompilerParams(

time: 47.8 us -> 42.3 us (0.88)
  Pallas kernels: 46 us -> 40.5 us
    pallas_call x1, Pallas kernels: 46 us -> 40.5 us  [local(): pl.pallas_call(functools.partial(kernel, n_dev), out_shape=jax.ShapeDtype...]
where the time goes in v2:
time: 42.3 us; the launch traced here: 42.1 us
  Pallas kernels  40.5 us (96%)
  local copies, waits for them, and re-layouts  1.57 us (4%)
    pallas_call x1, Pallas kernels, local(): pl.pallas_call(functools.partial(kernel, n_dev), out_shape=jax.ShapeDtype...  40.5 us
    unnamed x1, local copies, waits for them, and re-layouts  1.57 us

profile of v2, /device:TPU:0, one launch (start us, length us, event | category | flops | bytes accessed | tf_op | source)
XLA Modules:
  0.0 42.1 jit_solution(358154869436023070)
XLA Ops:
  0.0 40.5 %shard_map.82 = bf16[4,12288]{1,0:T(4,128)(2,1)} custom-call(bf16[4,12288]{1,0:T(4,128)(2,1)} %bitcast.10, s32[4,4]{1,0:T(4,128)} %bitcast.14, f32[1,12288]{1,0:T(1,128)} %bitcast.11, f32[1,12288]{1,0:T(1,128)} %bitcast.12, f32[1,256]{1,0:T(1,128)} %bitcast.15, f32[1,12288]{1,0:T(1,128)} %bitcast.13, bf16[4,3072,256]{2,1,0:T(8,128)(2,1)} %bitcast.8, ...), custom_call_target="tpu_custom_call" | custom-call | tf_op jit(solution)/shard_map/pallas_call | solution.py:281
  40.6 1.6 %copy.10 = bf16[4,1,12288]{2,0,1:T(4,128)(2,1)} copy(bf16[4,1,12288]{2,0,1:T(4,128)(2,1)} %bitcast.9) | data formatting | bytes 196608

commit v3 on v2

--- a/solution.py
+++ b/solution.py
@@ -52,7 +52,9 @@
     def source(d):
         return jnp.bitwise_xor(far, d) if fars & (fars - 1) == 0 else lax.rem(far + fars - d, fars)
 
-    far_peers = [(d, device(core, mid, other(d))) for d in range(1, fars)]
+    order = list(range(1, fars))
+    back_order = list(range(2, fars)) + [1] if fars > 1 else []
+    far_peers = [(d, device(core, mid, other(d))) for d in order]
     mid_peers = [(d, device(core, lax.rem(mid + d, mids), far)) for d in range(1, mids)]
     core_peers = [(d, device(lax.rem(core + d, cores), mid, far)) for d in range(1, cores)]
     barrier = pltpu.get_barrier_semaphore()
@@ -102,14 +104,14 @@
         here = rows.at[place(core, mid, source(d) if d else far), :, spans(c)]
         return [remote(here, here, mid_s.at[c, d, e], mid_r.at[c, d, e], peer) for e, peer in mid_peers]
 
-    far_copies, mid_copies, core_copies = [], [[] for _ in range(PARTS)], []
+    far_copies, mid_copies, core_copies = [], [[] for _ in range(PARTS)], [[] for _ in range(PARTS)]
     for c in range(PARTS):
         norm_part(c)
         if c == 0:
             pl.semaphore_wait(barrier, fars + mids + cores - 3)
         mid_copies[c] += spread(c, 0)
         here = rows.at[mine, :, spans(c)]
-        far_copies.append([remote(here, here, far_s.at[c, d], far_r.at[c, d], peer) for d, peer in far_peers])
+        far_copies.append({d: remote(here, here, far_s.at[c, d], far_r.at[c, d], peer) for d, peer in far_peers})
 
     for c in range(PARTS):
         for q in range(split):
@@ -149,15 +151,20 @@
 
         over_tiles(body)
 
-    for c in range(PARTS):
-        for d in range(1, fars):
-            far_copies[c][d - 1].wait_recv()
+    def share(c, e):
+        here = rows.at[pl.ds(place(core, lax.rem(mid + e, mids), 0), fars), :, spans(c)]
+        return [remote(here, here, core_s.at[c, e, d], core_r.at[c, e, d], peer) for d, peer in core_peers]
+
+    for c in range(PARTS):
+        for d in order:
+            far_copies[c][d].wait_recv()
             mid_copies[c] += spread(c, d)
+        core_copies[c] += share(c, 0)
     for c in range(PARTS):
         for copy in mid_copies[c]:
             copy.wait_recv()
-        here = rows.at[pl.ds(place(core, 0, 0), fars * mids), :, spans(c)]
-        core_copies.append([remote(here, here, core_s.at[c, d], core_r.at[c, d], peer) for d, peer in core_peers])
+        for e in range(1, mids):
+            core_copies[c] += share(c, e)
         for copy in core_copies[c]:
             copy.wait_recv()
         up_part(c)
@@ -182,7 +189,7 @@
             hid_cat[at, q * units:(q + 1) * units] = jnp.where(which == q, value, 0.0).astype(jnp.bfloat16)
 
     over_tiles(hidden_part)
-    for copies in far_copies + mid_copies + core_copies:
+    for copies in [list(got.values()) for got in far_copies] + mid_copies + core_copies:
         for copy in copies:
             copy.wait_send()
 
@@ -202,8 +209,7 @@
 
         over_tiles(body)
 
-    back_core, back_mid, back_far = [], {}, []
-    plane = fars * mids
+    back_core, back_mid, back_far = {}, {}, {}
 
     def chip_sum(c, m, f):
         at = slice(c * step, (c + 1) * step)
@@ -229,25 +235,32 @@
 
     for c in range(PARTS):
         down_part(c)
-        cols = pl.ds(LANES + c * step, step)
-        back_core.append([
-            remote(rows.at[pl.ds(place(lax.rem(core + d, cores), 0, 0), plane), :, cols],
-                   core_in.at[d - 1, :, :, pl.ds(c * step, step)], rcore_s.at[c, d], rcore_r.at[c, d], peer)
-            for d, peer in core_peers])
-    for c in range(PARTS):
-        for copy in back_core[c]:
-            copy.wait_recv()
-        for d in range(1, fars):
+        for e in list(range(1, mids)) + [0]:
+            m = lax.rem(mid + e, mids)
+            for d, peer in core_peers:
+                back_core[c, e, d] = remote(
+                    rows.at[pl.ds(place(lax.rem(core + d, cores), m, 0), fars), :, pl.ds(LANES + c * step, step)],
+                    core_in.at[d - 1, pl.ds(m * fars, fars), :, pl.ds(c * step, step)],
+                    rcore_s.at[c, e, d], rcore_r.at[c, e, d], peer)
+    for c in range(PARTS):
+        for e in range(1, mids):
+            for d in range(1, cores):
+                back_core[c, e, d].wait_recv()
+        for d in back_order:
             send_mid(c, d)
     for c in range(PARTS):
         send_mid(c, 0)
     for c in range(PARTS):
+        for d in range(1, cores):
+            back_core[c, 0, d].wait_recv()
+    for c in range(PARTS):
         cs = slice(c * step, (c + 1) * step)
-        for d, peer in far_peers:
+        for d in back_order:
+            peer = device(core, mid, other(d))
             far_out[d - 1, :, cs] = line_sum(c, d).astype(jnp.bfloat16)
             cols = pl.ds(c * step, step)
-            back_far.append(remote(far_out.at[d - 1, :, cols], far_in.at[d - 1, :, cols],
-                                   rfar_s.at[c, d], rfar_r.at[c, d], peer))
+            back_far[c, d] = remote(far_out.at[d - 1, :, cols], far_in.at[d - 1, :, cols],
+                                    rfar_s.at[c, d], rfar_r.at[c, d], peer)
     for c in range(PARTS):
         cs = slice(c * step, (c + 1) * step)
         far_own[:, cs] = line_sum(c, 0)
@@ -255,13 +268,13 @@
         cs = slice(c * step, (c + 1) * step)
         total = far_own[:, cs]
         for d in range(1, fars):
-            back_far[c * (fars - 1) + d - 1].wait_recv()
+            back_far[c, d].wait_recv()
             total = total + far_in[d - 1, :, cs].astype(jnp.float32)
         for q in range(split):
             at = slice(q * part + c * step, q * part + (c + 1) * step)
             mixed = hid[:, at].astype(jnp.float32) + down_bias[:, at] + total[q * row_count:(q + 1) * row_count]
             out[:, at] = mixed.astype(out.dtype)
-    for copies in back_core + [back_mid.values(), back_far]:
+    for copies in [back_core.values(), back_mid.values(), back_far.values()]:
         for copy in copies:
             copy.wait_send()
 
@@ -298,8 +311,8 @@
             dma((PARTS,)), dma((PARTS, split)),
             dma((PARTS, fars)), dma((PARTS, fars)),
             dma((PARTS, fars, mids)), dma((PARTS, fars, mids)),
-            dma((PARTS, cores)), dma((PARTS, cores)),
-            dma((PARTS, cores)), dma((PARTS, cores)),
+            dma((PARTS, mids, cores)), dma((PARTS, mids, cores)),
+            dma((PARTS, mids, cores)), dma((PARTS, mids, cores)),
             dma((PARTS, fars, mids)), dma((PARTS, fars, mids)),
             dma((PARTS, fars)), dma((PARTS, fars)),
         ],

time: 42.3 us -> 40.7 us (0.962)
  Pallas kernels: 40.5 us -> 39 us
    pallas_call x1, Pallas kernels: 40.5 us -> 39 us  [local(): pl.pallas_call(functools.partial(kernel, n_dev), out_shape=jax.ShapeDtype...]
where the time goes in v3:
time: 40.7 us; the launch traced here: 40.6 us
  Pallas kernels  39 us (96%)
  local copies, waits for them, and re-layouts  1.57 us (4%)
    pallas_call x1, Pallas kernels, local(): pl.pallas_call(functools.partial(kernel, n_dev), out_shape=jax.ShapeDtype...  39 us
    unnamed x1, local copies, waits for them, and re-layouts  1.57 us

profile of v3, /device:TPU:0, one launch (start us, length us, event | category | flops | bytes accessed | tf_op | source)
XLA Modules:
  0.0 40.6 jit_solution(1735898478290068927)
XLA Ops:
  0.0 39.0 %shard_map.82 = bf16[4,12288]{1,0:T(4,128)(2,1)} custom-call(bf16[4,12288]{1,0:T(4,128)(2,1)} %bitcast.10, s32[4,4]{1,0:T(4,128)} %bitcast.14, f32[1,12288]{1,0:T(1,128)} %bitcast.11, f32[1,12288]{1,0:T(1,128)} %bitcast.12, f32[1,256]{1,0:T(1,128)} %bitcast.15, f32[1,12288]{1,0:T(1,128)} %bitcast.13, bf16[4,3072,256]{2,1,0:T(8,128)(2,1)} %bitcast.8, ...), custom_call_target="tpu_custom_call" | custom-call | tf_op jit(solution)/shard_map/pallas_call | solution.py:294
  39.0 1.6 %copy.10 = bf16[4,1,12288]{2,0,1:T(4,128)(2,1)} copy(bf16[4,1,12288]{2,0,1:T(4,128)(2,1)} %bitcast.9) | data formatting | bytes 196608

commit v4 on v3

--- a/solution.py
+++ b/solution.py
@@ -242,7 +242,6 @@
                     rows.at[pl.ds(place(lax.rem(core + d, cores), m, 0), fars), :, pl.ds(LANES + c * step, step)],
                     core_in.at[d - 1, pl.ds(m * fars, fars), :, pl.ds(c * step, step)],
                     rcore_s.at[c, e, d], rcore_r.at[c, e, d], peer)
-    for c in range(PARTS):
         for e in range(1, mids):
             for d in range(1, cores):
                 back_core[c, e, d].wait_recv()

time: 40.7 us -> 40.8 us (level)
  no operation moved by 1% of the time
where the time goes in v4:
time: 40.8 us; the launch traced here: 40.7 us
  Pallas kernels  39.1 us (96%)
  local copies, waits for them, and re-layouts  1.57 us (4%)
    pallas_call x1, Pallas kernels, local(): pl.pallas_call(functools.partial(kernel, n_dev), out_shape=jax.ShapeDtype...  39.1 us
    unnamed x1, local copies, waits for them, and re-layouts  1.57 us

profile of v4, /device:TPU:0, one launch (start us, length us, event | category | flops | bytes accessed | tf_op | source)
XLA Modules:
  0.0 40.7 jit_solution(16663134020243349473)
XLA Ops:
  0.0 39.1 %shard_map.82 = bf16[4,12288]{1,0:T(4,128)(2,1)} custom-call(bf16[4,12288]{1,0:T(4,128)(2,1)} %bitcast.10, s32[4,4]{1,0:T(4,128)} %bitcast.14, f32[1,12288]{1,0:T(1,128)} %bitcast.11, f32[1,12288]{1,0:T(1,128)} %bitcast.12, f32[1,256]{1,0:T(1,128)} %bitcast.15, f32[1,12288]{1,0:T(1,128)} %bitcast.13, bf16[4,3072,256]{2,1,0:T(8,128)(2,1)} %bitcast.8, ...), custom_call_target="tpu_custom_call" | custom-call | tf_op jit(solution)/shard_map/pallas_call | solution.py:293
  39.1 1.6 %copy.10 = bf16[4,1,12288]{2,0,1:T(4,128)(2,1)} copy(bf16[4,1,12288]{2,0,1:T(4,128)(2,1)} %bitcast.9) | data formatting | bytes 196608
